TPU v7x, 512 devices: a whole 4x8x8 slice. The times are simulated.
512 devices in a mesh: sec: 32 (over x, y), head: 16 (over z, core).
Axes of the slice: x: 4, y: 8, z: 8, core: 2. Of those that a mesh axis runs over, the one named last changes fastest.
Arguments:
- tokens: bfloat16 [32768, 2048], P('sec', 'head'), may hold values from -6 to 6
- fresh_tokens: bfloat16 [1024, 2048], P(None, 'head'), may hold values from -6 to 6
- route_rows: int32 [32, 4, 128], P('sec'), may hold values from 0 to 255, as said below
- block_list: int32 [32, 4, 16], P('sec'), may hold values from 0 to 31, all different within a row
- norm_gain: float32 [32, 2048], P('sec'), may hold values from 0.25 to 1.75
- route_weight: bfloat16 [32, 2048], P('sec'), may hold values from -0.125 to 0.125
- w_query: bfloat16 [32, 2048, 2048], P('sec', None, 'head'), may hold values from -0.125 to 0.125
- w_key: bfloat16 [32, 2048, 2048], P('sec', None, 'head'), may hold values from -0.26367188 to 0.26367188
- w_value: bfloat16 [32, 2048, 2048], P('sec', None, 'head'), may hold values from -0.125 to 0.125
- w_out: bfloat16 [32, 2048, 2048], P('sec', None, 'head'), may hold values from -0.52734375 to 0.52734375
- cache_keys: bfloat16 [32, 4096, 2048], P('sec', None, 'head'), may hold values from -2400 to 2400
- cache_values: bfloat16 [32, 4096, 2048], P('sec', None, 'head'), may hold values from -6 to 6
Outputs:
- next_input: bfloat16 [32768, 2048], P('sec', 'head')
Inputs may be any that keep to these rules, and one draw needn't show every extreme that they name: `route_rows`: within one section and group the 128 entries are distinct row numbers of the group. `block_list`: each section's group names 16 distinct blocks.
All inputs are finite; a program needn't handle non-finite values.
Results may differ from a plain program's by a relative error of at most 0.017.
Values may be sent and summed in bfloat16 or wider, within the bound.
A program may use at most 64 MiB of HBM per device.

v0:
```python
import math

import jax
import jax.numpy as jnp
from jax import lax
from jax.sharding import Mesh
from jax.sharding import PartitionSpec as P

HEAD_DIM = 64
BLOCK = 128
HEAD = ("head_0", "head_1")


def gathered_by_axis(shard, axes, dim):
    if not axes:
        return shard
    nearer = lax.all_gather(shard, axes[-1], axis=dim, tiled=True)
    return gathered_by_axis(nearer, axes[:-1], dim)


def shifted_2(shard, axis, by):
    length = lax.axis_size(axis)
    pairs = [(i, i + by) for i in range(length) if 0 <= i + by < length]
    return lax.ppermute(shard, axis, pairs)


def attend_local(queries, key_rows, value_rows, row_index, cache_k, cache_v, picks):
    row_count, head_count, head_width = queries.shape
    group_count = picks.shape[0]
    score_scale = 1.0 / math.sqrt(head_width)
    chosen_keys = cache_k.reshape(-1, BLOCK, head_count, head_width)[picks].reshape(
        group_count, -1, head_count, head_width
    )
    chosen_values = cache_v.reshape(-1, BLOCK, head_count, head_width)[picks].reshape(
        group_count, -1, head_count, head_width
    )
    query_groups = queries.reshape(group_count, -1, head_count, head_width)
    cache_scores = (
        jnp.einsum("crhd,ckhd->chrk", query_groups, chosen_keys, preferred_element_type=jnp.float32)
        * score_scale
    )
    local_scores = (
        jnp.einsum("qhd,khd->hqk", queries, key_rows, preferred_element_type=jnp.float32)
        * score_scale
    )
    visible = row_index[None, :] <= row_index[:, None]
    local_scores = jnp.where(visible[None], local_scores, -jnp.inf)
    cache_max = jnp.transpose(jnp.max(cache_scores, axis=-1), (1, 0, 2)).reshape(
        head_count, row_count
    )
    row_max = jnp.maximum(cache_max, jnp.max(local_scores, axis=-1))
    group_max = jnp.transpose(row_max.reshape(head_count, group_count, -1), (1, 0, 2))
    cache_weights = jnp.exp(cache_scores - group_max[..., None])
    local_weights = jnp.exp(local_scores - row_max[..., None])
    cache_sum = jnp.transpose(jnp.sum(cache_weights, axis=-1), (1, 0, 2)).reshape(
        head_count, row_count
    )
    denom_sum = cache_sum + jnp.sum(local_weights, axis=-1)
    from_cache = jnp.einsum(
        "chrk,ckhd->crhd",
        cache_weights.astype(jnp.bfloat16),
        chosen_values,
        preferred_element_type=jnp.float32,
    ).reshape(row_count, head_count, head_width)
    from_local = jnp.einsum(
        "hqk,khd->qhd",
        local_weights.astype(jnp.bfloat16),
        value_rows,
        preferred_element_type=jnp.float32,
    )
    attended = (from_cache + from_local) / jnp.transpose(denom_sum)[:, :, None]
    return attended.astype(jnp.bfloat16).reshape(row_count, head_count * head_width)


def body(
    tokens,
    fresh_tokens,
    route_rows,
    block_list,
    norm_gain,
    route_weight,
    w_query,
    w_key,
    w_value,
    w_out,
    cache_keys,
    cache_values,
):
    group_count = route_rows.shape[1]
    group_rows = tokens.shape[0] // group_count
    row_index = (
        route_rows[0] + group_rows * jnp.arange(group_count, dtype=jnp.int32)[:, None]
    ).reshape(-1)
    own_rows = jnp.take(tokens, row_index, axis=0)
    picked_rows = gathered_by_axis(own_rows, HEAD, 1)
    picked = picked_rows.astype(jnp.float32)
    mean_square = jnp.mean(picked * picked, axis=-1, keepdims=True)
    normed = (picked * lax.rsqrt(mean_square + 1e-05) * norm_gain[0][None, :]).astype(jnp.bfloat16)
    gate_value = jax.nn.sigmoid(
        jnp.dot(normed, route_weight[0], preferred_element_type=jnp.float32)
    )
    local_heads = w_query.shape[2] // HEAD_DIM
    queries = (
        jnp.dot(normed, w_query[0], preferred_element_type=jnp.float32)
        .astype(jnp.bfloat16)
        .reshape(-1, local_heads, HEAD_DIM)
    )
    key_rows = (
        jnp.dot(normed, w_key[0], preferred_element_type=jnp.float32)
        .astype(jnp.bfloat16)
        .reshape(-1, local_heads, HEAD_DIM)
    )
    value_rows = (
        jnp.dot(normed, w_value[0], preferred_element_type=jnp.float32)
        .astype(jnp.bfloat16)
        .reshape(-1, local_heads, HEAD_DIM)
    )
    attended = attend_local(
        queries, key_rows, value_rows, row_index, cache_keys[0], cache_values[0], block_list[0]
    )
    output_rows = w_out[0]
    branch = jnp.dot(
        lax.all_gather(attended, HEAD, axis=1, tiled=True),
        output_rows,
        preferred_element_type=jnp.float32,
    )
    own_columns = jnp.take(tokens, row_index, axis=0).astype(jnp.float32)
    updated = (own_columns + gate_value[:, None] * branch).astype(jnp.bfloat16)
    result = tokens.at[row_index].set(updated)
    shifted = shifted_2(result, "sec", 1)
    return jnp.where(lax.axis_index("sec") == 0, fresh_tokens, shifted)


def solution(mesh):
    torus = Mesh(mesh.devices.reshape(mesh.shape["sec"], 8, 2), ("sec", "head_0", "head_1"))
    in_specs = (
        P("sec", HEAD),
        P(None, HEAD),
        P("sec", None, None),
        P("sec", None, None),
        P("sec", None),
        P("sec", None),
        P("sec", None, HEAD),
        P("sec", None, HEAD),
        P("sec", None, HEAD),
        P("sec", None, HEAD),
        P("sec", None, HEAD),
        P("sec", None, HEAD),
    )
    out_specs = P("sec", HEAD)
    return jax.shard_map(body, mesh=torus, in_specs=in_specs, out_specs=out_specs, check_vma=False)
```

profile of v0, /device:TPU:2, one launch (start us, length us, event | category | flops | bytes accessed | tf_op | source)
XLA Modules:
  0.0 152.1 jit_solution(10076083262525095151)
XLA Ops:
  6.5 0.0 copy-start
  6.5 0.0 copy-start.10
  6.5 0.0 copy-start.4
  6.5 0.0 all-gather.3.cloned.1.call-start
  6.5 1.1 copy.65
  7.6 0.8 compare_and_fusion
  8.4 1.3 gather_fusion.2
  9.7 0.1 broadcast_select_fusion.1
  9.9 2.1 %all_gather.9 = bf16[512,256]{1,0:T(8,128)(2,1)} all-gather(bf16[512,128]{1,0:T(8,128)(2,1)S(1)} %broadcast_select_fusion.1), channel_id=1, replica_groups=mesh['sec'=32,'head_0'=8,'head_1'=2] {'head_1'}, dimensions={1}, use_global_device_ids=true | all-gather | bytes 393216 | tf_op jit(solution)/shard_map/all_gather | solution.py:17
  12.0 0.0 all-gather.3.cloned.1.call-update
  12.0 0.0 all-gather.5.cloned.1.call-start
  12.1 0.0 copy-done.10
  12.1 0.1 reshape.179
  12.2 0.0 copy-done.4
  12.2 1.8 %reshape.212 = bf16[32,128,2,64]{3,2,1,0:T(2,128)(2,1)} reshape(bf16[1,4096,128]{2,1,0:T(8,128)(2,1)S(1)} %copy-done.4) | data formatting | bytes 2097152 | tf_op jit(solution)/shard_map/reshape;squeeze | solution.py:31
  14.0 5.0 %copy.37 = bf16[32,128,2,64]{1,3,2,0:T(8,128)(2,1)S(1)} copy(bf16[32,128,2,64]{3,2,1,0:T(2,128)(2,1)} %reshape.212) | data formatting | bytes 2097152 | tf_op jit(solution)/shard_map/reshape;squeeze | solution.py:31
  19.1 2.1 %gather_fusion.1 = bf16[64,128,2,64]{1,3,2,0:T(8,128)(2,1)} fusion(bf16[32,128,2,64]{1,3,2,0:T(8,128)(2,1)S(1)} %copy.37, s32[1024]{0:T(1024)S(1)} %pad_clamp_fusion), kind=kCustom, calls=%fused_computation.2 | custom fusion | bytes 4194560 | tf_op jit(solution)/shard_map/gather | solution.py:31
  21.2 2.9 %copy.38 = bf16[64,128,2,64]{1,0,3,2:T(8,128)(2,1)S(1)} copy(bf16[64,128,2,64]{1,3,2,0:T(8,128)(2,1)} %gather_fusion.1) | data formatting | bytes 4194304 | tf_op jit(solution)/shard_map/gather | solution.py:31
  24.1 2.0 %reshape.161 = bf16[4,2048,2,64]{1,0,3,2:T(4,128)(2,1)} reshape(bf16[64,128,2,64]{1,0,3,2:T(8,128)(2,1)S(1)} %copy.38) | data formatting | bytes 4194304 | tf_op jit(solution)/shard_map/reshape | solution.py:31
  26.2 5.0 %reshape.211 = bf16[32,128,2,64]{3,2,1,0:T(2,128)(2,1)} reshape(bf16[1,4096,128]{2,1,0:T(8,128)(2,1)} %param.25) | data formatting | bytes 2097152 | tf_op jit(solution)/shard_map/reshape;squeeze | solution.py:34
  31.2 5.1 %copy.34 = bf16[32,128,2,64]{1,3,2,0:T(8,128)(2,1)S(1)} copy(bf16[32,128,2,64]{3,2,1,0:T(2,128)(2,1)} %reshape.211) | data formatting | bytes 2097152 | tf_op jit(solution)/shard_map/reshape;squeeze | solution.py:34
  36.2 2.1 %gather_fusion = bf16[64,128,2,64]{1,3,2,0:T(8,128)(2,1)} fusion(bf16[32,128,2,64]{1,3,2,0:T(8,128)(2,1)S(1)} %copy.34, s32[1024]{0:T(1024)S(1)} %pad_clamp_fusion), kind=kCustom, calls=%fused_computation.1 | custom fusion | bytes 4194560 | tf_op jit(solution)/shard_map/gather | solution.py:34
  38.4 3.0 %copy.35 = bf16[64,128,2,64]{1,0,3,2:T(8,128)(2,1)S(1)} copy(bf16[64,128,2,64]{1,3,2,0:T(8,128)(2,1)} %gather_fusion) | data formatting | bytes 4194304 | tf_op jit(solution)/shard_map/gather | solution.py:34
  41.4 2.1 %reshape.160 = bf16[4,2048,2,64]{1,0,3,2:T(4,128)(2,1)} reshape(bf16[64,128,2,64]{1,0,3,2:T(8,128)(2,1)S(1)} %copy.35) | data formatting | bytes 4194304 | tf_op jit(solution)/shard_map/reshape | solution.py:34
  43.5 0.0 copy-start.7
  43.5 0.2 broadcast_compare_fusion
  43.7 23.5 %all-gather.3.cloned.1.call-done = bf16[512,2048]{1,0:T(8,128)(2,1)} async-done(((bf16[512,256]{1,0:T(8,128)(2,1)}), bf16[512,2048]{1,0:T(8,128)(2,1)}) %all-gather.3.cloned.1.call-update) | async-done | bytes 2097168 | tf_op jit(solution)/shard_map/all_gather | solution.py:17
  67.2 0.0 copy-start.3
  67.2 2.2 %fusion.2 = f32[512]{0:T(512)S(1)} fusion(bf16[512,2048]{1,0:T(8,128)(2,1)} %all-gather.3.cloned.1.call-done), kind=kLoop, calls=%fused_computation.10 | loop fusion | flops 3145216 | bytes 2099200 | tf_op jit(solution)/shard_map/reduce_sum | solution.py:97
  69.5 0.0 copy-done.7
  69.5 0.0 copy-done.3
  69.5 0.5 fusion.4
  70.0 0.0 copy-done
  70.0 0.8 convolution_convert_fusion.2
  70.9 0.0 copy-start.2
  70.9 2.0 %convolution_convert_fusion.1 = bf16[512,128]{0,1:T(8,128)(2,1)S(1)} fusion(bf16[512,2048]{1,0:T(8,128)(2,1)S(1)} %fusion.4, bf16[1,2048,128]{2,1,0:T(8,128)(2,1)} %param.21), kind=kOutput, calls=%fused_computation.32 | convolution fusion | flops 268500992 | bytes 2752512 | tf_op jit(solution)/shard_map/dot_general | solution.py:109
  72.9 0.0 copy-done.2
  72.9 3.4 %multiply_reduce_fusion = (f32[4,2,128]{2,1,0:T(2,128)S(1)}, f32[4,2,128,2048]{3,2,1,0:T(8,128)S(1)}) fusion(bf16[4,2048,2,64]{1,0,3,2:T(4,128)(2,1)S(1)} %copy-done.2, bf16[4,128,2,64]{1,0,3,2:T(4,128)(2,1)S(1)} %reshape_reshape.3), kind=kOutput, calls=%fused_computation.5 | convolution fusion | flops 272628736 | bytes 10620928 | tf_op jit(solution)/shard_map/crhd,ckhd->chrk/dot_general | solution.py:39
  76.3 0.0 copy-start.5
  76.3 0.6 fusion.12
  77.0 0.4 copy-done.5
  77.4 0.8 convolution_convert_fusion
  78.2 0.0 copy-start.1
  78.2 1.6 %fusion = f32[4,2,128]{2,1,0:T(2,128)S(1)} fusion(f32[4,2,128,2048]{3,2,1,0:T(8,128)S(1)} %get-tuple-element.11, f32[4,2,128]{2,1,0:T(2,128)S(1)} %fusion.37), kind=kLoop, calls=%fused_computation.6 | loop fusion | flops 6290432 | bytes 8396800 | tf_op jit(solution)/shard_map/reduce_sum | solution.py:55
  79.8 0.0 copy-done.1
  79.9 3.6 %fusion.18 = f32[4,2,8,8,128]{4,3,2,1,0:T(8,128)S(1)} fusion(f32[4,2,128,2048]{3,2,1,0:T(8,128)S(1)} %get-tuple-element.11, f32[4,2,128]{2,1,0:T(2,128)S(1)} %fusion.37, bf16[4,2048,2,64]{1,0,3,2:T(4,128)(2,1)S(1)} %copy-done.1), kind=kOutput, calls=%fused_computation.29 | convolution fusion | flops 274726912 | bytes 10752000 | tf_op jit(solution)/shard_map/chrk,ckhd->crhd/dot_general | solution.py:59
  83.5 0.5 fusion.13
  84.0 0.0 copy-start.9
  84.0 0.0 copy-start.8
  84.0 1.4 fusion.24
  85.4 0.0 all-gather.5.cloned.1.call-update
  85.4 0.1 add.84
  85.5 0.0 copy-done.9
  85.5 0.0 copy-done.8
  85.5 0.6 fusion.34
  86.2 0.0 copy-start.6
  86.2 41.6 %all-gather.5.cloned.1.call-done = bf16[512,2048]{0,1:T(8,128)(2,1)} async-done(((bf16[512,128]{0,1:T(8,128)(2,1)}), bf16[512,2048]{0,1:T(8,128)(2,1)}) %all-gather.5.cloned.1.call-update) | async-done | bytes 2097168 | tf_op jit(solution)/shard_map/all_gather | solution.py:123
  127.7 2.4 %fusion.23 = bf16[512,128]{1,0:T(8,128)(2,1)S(1)} fusion(bf16[512,2048]{0,1:T(8,128)(2,1)} %all-gather.5.cloned.1.call-done, bf16[1,2048,128]{2,1,0:T(8,128)(2,1)} %param.23, bf16[512,128]{1,0:T(8,128)(2,1)S(1)} %broadcast_select_fusion.1, f32[512]{0:T(512)S(1)} %add_divide_fusion), kind=kOutput, calls=%fused_computation.30 | convolution fusion | flops 268697600 | bytes 2885632 | tf_op jit(solution)/shard_map/dot_general | solution.py:122
  130.2 1.9 %scatter_fusion = bf16[1024,128]{1,0:T(8,128)(2,1)S(1)} fusion(bf16[1024,128]{1,0:T(8,128)(2,1)S(1)} %copy.65, s32[512]{0:T(512)S(1)} %bitcast.90, bf16[512,128]{1,0:T(8,128)(2,1)S(1)} %fusion.23), kind=kCustom, calls=%fused_computation.3 | custom fusion | bytes 395264 | tf_op jit(solution)/shard_map/scatter | solution.py:129
  132.1 3.4 %collective-permute-start = (bf16[1024,128]{1,0:T(8,128)(2,1)S(1)}, bf16[1024,128]{1,0:T(8,128)(2,1)S(1)}, u32[]{:S(2)}, u32[]{:S(2)}) collective-permute-start(bf16[1024,128]{1,0:T(8,128)(2,1)S(1)} %scatter_fusion), channel_id=1, source_target_pairs={{0,16},{16,32},{32,48},{48,64},{64,80},{80,96},{96,112},{112,128},... | collective-permute-start | bytes 786440 | tf_op jit(solution)/shard_map/ppermute | solution.py:24
  135.5 9.1 %collective-permute-done = bf16[1024,128]{1,0:T(8,128)(2,1)S(1)} collective-permute-done((bf16[1024,128]{1,0:T(8,128)(2,1)S(1)}, bf16[1024,128]{1,0:T(8,128)(2,1)S(1)}, u32[]{:S(2)}, u32[]{:S(2)}) %collective-permute-start) | collective-permute-done | bytes 262176 | tf_op jit(solution)/shard_map/ppermute | solution.py:24
  144.6 0.0 copy-done.6
  144.6 0.7 broadcast_select_fusion
  (12 shorter events, 0.1 us)
Async XLA Ops:
  6.5 63.5 %copy-start = (bf16[1,2048,128]{2,1,0:T(8,128)(2,1)S(1)}, bf16[1,2048,128]{2,1,0:T(8,128)(2,1)}, u32[]{:S(2)}) copy-start(bf16[1,2048,128]{2,1,0:T(8,128)(2,1)} %param.20) | copy-start | bytes 1572868
  6.5 5.5 %copy-start.10 = (s32[1,4,16]{2,1,0:T(4,128)S(1)}, s32[1,4,16]{2,1,0:T(4,128)}, u32[]{:S(2)}) copy-start(s32[1,4,16]{2,1,0:T(4,128)} %param.17) | copy-start | bytes 772
  6.5 5.7 %copy-start.4 = (bf16[1,4096,128]{2,1,0:T(8,128)(2,1)S(1)}, bf16[1,4096,128]{2,1,0:T(8,128)(2,1)}, u32[]{:S(2)}) copy-start(bf16[1,4096,128]{2,1,0:T(8,128)(2,1)} %param.24) | copy-start | bytes 3145732
  6.5 60.7 %all-gather.3.cloned.1.call-start = ((), (), s32[]{:S(2)}) async-start(), calls=%async_computation | async-start | bytes 2359296 | tf_op jit(solution)/shard_map/all_gather | solution.py:17
  12.0 115.7 %all-gather.5.cloned.1.call-start = ((), (), s32[]{:S(2)}) async-start(), calls=%async_computation.1 | async-start | bytes 2228224 | tf_op jit(solution)/shard_map/all_gather | solution.py:123
  43.5 26.0 %copy-start.7 = (f32[1,2048]{1,0:T(1,128)S(1)}, f32[1,2048]{1,0:T(1,128)}, u32[]{:S(2)}) copy-start(f32[1,2048]{1,0:T(1,128)} %param.18) | copy-start | bytes 24580
  67.2 2.2 %copy-start.3 = (bf16[512,2048]{1,0:T(8,128)(2,1)S(1)}, bf16[512,2048]{1,0:T(8,128)(2,1)}, u32[]{:S(2)}) copy-start(bf16[512,2048]{1,0:T(8,128)(2,1)} %all-gather.3.cloned.1.call-done) | copy-start | bytes 6291460
  70.9 2.0 %copy-start.2 = (bf16[4,2048,2,64]{1,0,3,2:T(4,128)(2,1)S(1)}, bf16[4,2048,2,64]{1,0,3,2:T(4,128)(2,1)}, u32[]{:S(2)}) copy-start(bf16[4,2048,2,64]{1,0,3,2:T(4,128)(2,1)} %reshape.161) | copy-start | bytes 6291460
  76.3 1.0 copy-start.5
  78.2 1.7 %copy-start.1 = (bf16[4,2048,2,64]{1,0,3,2:T(4,128)(2,1)S(1)}, bf16[4,2048,2,64]{1,0,3,2:T(4,128)(2,1)}, u32[]{:S(2)}) copy-start(bf16[4,2048,2,64]{1,0,3,2:T(4,128)(2,1)} %reshape.160) | copy-start | bytes 6291460
  84.0 1.5 copy-start.9
  84.0 1.5 copy-start.8
  86.2 58.4 %copy-start.6 = (bf16[1024,128]{1,0:T(8,128)(2,1)S(1)}, bf16[1024,128]{1,0:T(8,128)(2,1)}, u32[]{:S(2)}) copy-start(bf16[1024,128]{1,0:T(8,128)(2,1)} %param.15) | copy-start | bytes 786436
  132.1 12.5 %collective-permute-start = (bf16[1024,128]{1,0:T(8,128)(2,1)S(1)}, bf16[1024,128]{1,0:T(8,128)(2,1)S(1)}, u32[]{:S(2)}, u32[]{:S(2)}) collective-permute-start(bf16[1024,128]{1,0:T(8,128)(2,1)S(1)} %scatter_fusion), channel_id=1, source_target_pairs={{0,16},{16,32},{32,48},{48,64},{64,80},{80,96},{96,112},{112,128},... | collective-permute-start | bytes 786440 | tf_op jit(solution)/shard_map/ppermute | solution.py:24
Sparse Core Ops, SparseCore 0:
  12.2 55.0 all-gather.2
  85.5 42.1 all-gather.4
where the time goes:
time: 153 us; the launch traced here: 152 us
  waiting for transfers between devices  74.2 us (48%)
  local copies, waits for them, and re-layouts  36.2 us (24%)
  matrix products  15.7 us (10%)
  between operations  13.7 us (9%)
  other arithmetic  6.82 us (4%)
  starting transfers between devices  3.44 us (2%)
  blocking collectives  2.13 us (1%)
    all_gather x1, waiting for transfers between devices, body(): lax.all_gather(attended, HEAD, axis=1, tiled=True)  41.6 us
    all_gather x1, waiting for transfers between devices, gathered_by_axis(): nearer = lax.all_gather(shard, axes[-1], axis=dim, tiled=True)  23.5 us
    another operation x2, local copies, waits for them, and re-layouts, attend_local(): cache_v.reshape(-1, BLOCK, head_count, head_width)[picks]  10 us
    ppermute x1, waiting for transfers between devices, shifted_2(): return lax.ppermute(shard, axis, pairs)  9.06 us
    another operation x2, local copies, waits for them, and re-layouts, attend_local(): cache_k.reshape(-1, BLOCK, head_count, head_width)[picks]  6.87 us
    gather x2, local copies, waits for them, and re-layouts, attend_local(): cache_v.reshape(-1, BLOCK, head_count, head_width)[picks]  5.13 us
    gather x2, local copies, waits for them, and re-layouts, attend_local(): cache_k.reshape(-1, BLOCK, head_count, head_width)[picks]  5.07 us
    dot_general x1, matrix products, attend_local(): jnp.einsum('chrk,ckhd->crhd', cache_weights.astype(jnp.bfloat16), chosen_...  3.63 us
  transfers between devices with their start and end apart: 3, of which 3 were waited for; matrix products, arithmetic and copies ran while one was open for 21% of the time, Pallas kernels for 0%

commit v1 on v0

v1 whole, which is shorter than its diff:
```python
import functools

import jax
import jax.numpy as jnp
from jax import lax
from jax.experimental import pallas as pl
from jax.experimental.pallas import tpu as pltpu
from jax.sharding import PartitionSpec as P

HEAD_DIM = 64
BLOCK = 128
WIDTH = 128
MESH = pl.DeviceIdType.MESH
F32 = jnp.float32
BF16 = jnp.bfloat16


def dot(a, b, dims=((1,), (0,))):
    return lax.dot_general(a, b, (dims, ((), ())), preferred_element_type=F32)


def kernel(
    sections,
    chips,
    blocks_ref,
    route_hbm,
    gain_hbm,
    router_hbm,
    tokens_hbm,
    wq_hbm,
    wk_hbm,
    wv_hbm,
    wo_hbm,
    ck_hbm,
    cv_hbm,
    out_ref,
    route,
    gain,
    router,
    tokens,
    wcat,
    wo,
    ck,
    cv,
    xg,
    ag,
    normed,
    scores,
    klocal,
    vlocal,
    gates,
    place,
    passed,
    result,
    load_sem,
    ring_send,
    ring_recv,
    pair_send,
    pair_recv,
    next_send,
    next_recv,
):
    groups, routed = route.shape
    group_rows = tokens.shape[0] // groups
    half = chips // 2
    picked_blocks = blocks_ref.shape[1]
    shards = 2 * chips
    width = shards * WIDTH

    sec = lax.axis_index("sec")
    head = lax.axis_index("head")
    chip = head // 2
    core = head % 2
    up = ((chip + 1) % chips) * 2 + core
    down = ((chip + chips - 1) % chips) * 2 + core
    pair = chip * 2 + 1 - core
    after = (sec + 1) % sections
    before = (sec + sections - 1) % sections

    loads = [
        pltpu.make_async_copy(a, b, load_sem.at[i])
        for i, (a, b) in enumerate(
            (
                (route_hbm, route),
                (tokens_hbm, tokens),
                (router_hbm, router),
                (gain_hbm, gain),
                (wq_hbm, wcat.at[:, pl.ds(0, WIDTH)]),
                (wk_hbm, wcat.at[:, pl.ds(WIDTH, WIDTH)]),
                (wv_hbm, wcat.at[:, pl.ds(2 * WIDTH, WIDTH)]),
                (ck_hbm, ck),
                (cv_hbm, cv),
                (wo_hbm, wo),
            )
        )
    ]
    for load in loads:
        load.start()

    barrier = pltpu.get_barrier_semaphore()
    for there in (
        {"head": up},
        {"head": down},
        {"head": pair},
        {"sec": after},
        {"sec": before},
    ):
        pl.semaphore_signal(barrier, inc=1, device_id=there, device_id_type=MESH)

    bufs = (xg, ag)

    def ring_copy(p, g, slot, hop, way):
        ref = bufs[p].at[g, slot]
        if hop == half:
            ref = ref.at[pl.ds(way * (routed // 2), routed // 2)]
        i = 2 * (hop - 1) + way
        return pltpu.make_async_remote_copy(
            src_ref=ref,
            dst_ref=ref,
            send_sem=ring_send.at[p, g, i],
            recv_sem=ring_recv.at[p, g, i],
            device_id={"head": up if way == 0 else down},
            device_id_type=MESH,
        )

    def pair_copy(p, g, slot, i):
        ref = bufs[p].at[g, slot]
        return pltpu.make_async_remote_copy(
            src_ref=ref,
            dst_ref=ref,
            send_sem=pair_send.at[p, g, i],
            recv_sem=pair_recv.at[p, g, i],
            device_id={"head": pair},
            device_id_type=MESH,
        )

    def arrived(hop, way):
        off = chips - hop if way == 0 else hop
        return ((chip + off) % chips) * 2 + core

    def send_own(p, g):
        for way in (0, 1):
            ring_copy(p, g, head, 1, way).start()
        pair_copy(p, g, head, 0).start()

    def ring_step(p, g, hop):
        for way in (0, 1):
            slot = arrived(hop, way)
            ring_copy(p, g, slot, hop, way).wait_recv()
            if hop < half:
                ring_copy(p, g, slot, hop + 1, way).start()
                pair_copy(p, g, slot, 2 * hop - 1 + way).start()
        if hop == half:
            pair_copy(p, g, arrived(hop, 0), 2 * half - 1).start()

    def pair_wait(p, g):
        for i in range(2 * half):
            pair_copy(p, g, pair, i).wait_recv()

    def drain(p, g):
        for hop in range(1, half + 1):
            for way in (0, 1):
                ring_copy(p, g, head, hop, way).wait_send()
        for i in range(2 * half):
            pair_copy(p, g, head, i).wait_send()

    def next_copy(g):
        return pltpu.make_async_remote_copy(
            src_ref=result.at[pl.ds(g * group_rows, group_rows)],
            dst_ref=out_ref.at[pl.ds(g * group_rows, group_rows)],
            send_sem=next_send.at[g],
            recv_sem=next_recv.at[g],
            device_id={"sec": after},
            device_id_type=MESH,
        )

    def pick(g):
        chosen = route[g : g + 1, :]
        rows = lax.broadcasted_iota(jnp.int32, (group_rows, routed), 0)
        one_hot = jnp.where(rows == chosen, 1.0, 0.0).astype(F32)
        here = one_hot.astype(BF16)
        place[g] = here
        mine = tokens[pl.ds(g * group_rows, group_rows), :]
        xg[g, head] = dot(here, mine, ((0,), (0,))).astype(BF16)
        used = jnp.max(one_hot, axis=1, keepdims=True)
        passed[pl.ds(g * group_rows, group_rows), :] = jnp.where(
            used > 0.0, 0.0, mine.astype(F32)
        ).astype(BF16)

    def project(g):
        total = jnp.zeros((routed, WIDTH), F32)
        for s in range(shards):
            x = xg[g, s].astype(F32)
            total += x * x
        mean = jnp.sum(total, axis=1, keepdims=True) * (1.0 / width)
        scale = lax.rsqrt(mean + 1e-05)
        for s in range(shards):
            lanes = slice(s * WIDTH, (s + 1) * WIDTH)
            x = xg[g, s].astype(F32)
            normed[:, lanes] = (x * scale * gain[:, lanes]).astype(BF16)
        y = dot(normed[...], wcat[...])
        gates[g] = jax.nn.sigmoid(y[:, 3 * WIDTH :])
        klocal[g] = y[:, WIDTH : 2 * WIDTH].astype(BF16)
        vlocal[g] = y[:, 2 * WIDTH : 3 * WIDTH].astype(BF16)
        return y[:, :WIDTH].astype(BF16)

    def attend(g, q):
        lane = lax.broadcasted_iota(jnp.int32, (routed, WIDTH), 1)
        first = lane < HEAD_DIM
        qs = q.astype(F32) * 0.125
        both = jnp.concatenate(
            [jnp.where(first, qs, 0.0), jnp.where(first, 0.0, qs)], axis=0
        ).astype(BF16)
        starts = [blocks_ref[g, i] for i in range(picked_blocks)]
        kinds = [(ck, cv, s) for s in starts] + [(klocal, vlocal, c) for c in range(g + 1)]

        r = jnp.broadcast_to(route[g : g + 1, :].astype(F32), (routed, routed))
        visible = r <= jnp.transpose(r)
        visible = jnp.concatenate([visible, visible], axis=0)
        spans = [kinds[i : i + 2] for i in range(0, len(kinds), 2)]
        top = None
        at = 0
        where = []
        for span in spans:
            keys = jnp.concatenate([k[i] for k, _, i in span], axis=0)
            s = dot(both, keys, ((1,), (1,)))
            for j, (k, _, i) in enumerate(span):
                part = s[:, j * BLOCK : (j + 1) * BLOCK]
                if k is klocal and i == g:
                    part = jnp.where(visible, part, -jnp.inf)
                scores[:, at + j * BLOCK : at + (j + 1) * BLOCK] = part
                top = part if top is None else jnp.maximum(top, part)
            where.append((at, BLOCK * len(span)))
            at += BLOCK * len(span)
        high = jnp.max(top, axis=1, keepdims=True)
        total = jnp.zeros((2 * routed, WIDTH), F32)
        acc = jnp.zeros((2 * routed, WIDTH), F32)
        for (at, size), span in zip(where, spans):
            w = jnp.exp(scores[:, at : at + size] - high)
            for j in range(len(span)):
                total += w[:, j * BLOCK : (j + 1) * BLOCK]
            values = jnp.concatenate([v[i] for _, v, i in span], axis=0)
            acc += dot(w.astype(BF16), values)
        denom = jnp.sum(total, axis=1, keepdims=True)
        ratio = acc / denom
        ag[g, head] = jnp.where(first, ratio[:routed], ratio[routed:]).astype(BF16)

    def finish(g):
        attended = jnp.concatenate([ag[g, s] for s in range(shards)], axis=1)
        branch = dot(attended, wo[...])
        updated = (xg[g, head].astype(F32) + gates[g] * branch).astype(BF16)
        rows = pl.ds(g * group_rows, group_rows)
        moved = dot(place[g], updated)
        result[rows, :] = (moved + passed[rows, :].astype(F32)).astype(BF16)
        next_copy(g).start()

    loads[0].wait()
    loads[1].wait()
    for g in range(groups):
        pick(g)
    pl.semaphore_wait(barrier, 5)
    for g in range(groups):
        send_own(0, g)

    loads[2].wait()
    for s in range(shards):
        lanes = slice(s * WIDTH, (s + 1) * WIDTH)
        wide = jnp.broadcast_to(router[:, lanes].astype(F32), (WIDTH, WIDTH))
        wcat[lanes, 3 * WIDTH :] = jnp.transpose(wide).astype(BF16)

    for hop in range(1, half + 1):
        for g in range(groups):
            ring_step(0, g, hop)
    for load in loads[3:]:
        load.wait()

    for t in range(groups + half):
        if t < groups:
            pair_wait(0, t)
            attend(t, project(t))
            send_own(1, t)
        for g in range(groups):
            if 1 <= t - g <= half:
                ring_step(1, g, t - g)
        done = t - half
        if done >= 0:
            pair_wait(1, done)
            finish(done)

    for g in range(groups):
        drain(0, g)
        drain(1, g)
        next_copy(g).wait()


def body(
    tokens,
    fresh_tokens,
    route_rows,
    block_list,
    norm_gain,
    route_weight,
    w_query,
    w_key,
    w_value,
    w_out,
    cache_keys,
    cache_values,
):
    sections = lax.axis_size("sec")
    shards = lax.axis_size("head")
    chips = shards // 2
    half = chips // 2
    groups, routed = route_rows.shape[1:]
    rows = tokens.shape[0]
    width = shards * WIDTH
    cached = cache_keys.shape[1] // BLOCK
    picked = block_list.shape[2] * BLOCK
    dma = pltpu.SemaphoreType.DMA
    hbm = pl.BlockSpec(memory_space=pl.ANY)
    shifted = pl.pallas_call(
        functools.partial(kernel, sections, chips),
        out_shape=jax.ShapeDtypeStruct((rows, WIDTH), BF16),
        in_specs=[pl.BlockSpec(memory_space=pltpu.SMEM)] + [hbm] * 10,
        out_specs=hbm,
        scratch_shapes=[
            pltpu.VMEM((groups, routed), jnp.int32),
            pltpu.VMEM((1, width), F32),
            pltpu.VMEM((1, width), BF16),
            pltpu.VMEM((rows, WIDTH), BF16),
            pltpu.VMEM((width, 4 * WIDTH), BF16),
            pltpu.VMEM((width, WIDTH), BF16),
            pltpu.VMEM((cached, BLOCK, WIDTH), BF16),
            pltpu.VMEM((cached, BLOCK, WIDTH), BF16),
            pltpu.VMEM((groups, shards, routed, WIDTH), BF16),
            pltpu.VMEM((groups, shards, routed, WIDTH), BF16),
            pltpu.VMEM((routed, width), BF16),
            pltpu.VMEM((2 * routed, picked + groups * routed), F32),
            pltpu.VMEM((groups, routed, WIDTH), BF16),
            pltpu.VMEM((groups, routed, WIDTH), BF16),
            pltpu.VMEM((groups, routed, WIDTH), F32),
            pltpu.VMEM((groups, rows // groups, routed), BF16),
            pltpu.VMEM((rows, WIDTH), BF16),
            pltpu.VMEM((rows, WIDTH), BF16),
            dma((10,)),
            dma((2, groups, 2 * half)),
            dma((2, groups, 2 * half)),
            dma((2, groups, 2 * half)),
            dma((2, groups, 2 * half)),
            dma((groups,)),
            dma((groups,)),
        ],
        compiler_params=pltpu.CompilerParams(
            collective_id=0, has_side_effects=True, vmem_limit_bytes=60 << 20
        ),
    )(
        block_list[0],
        route_rows[0],
        norm_gain,
        route_weight,
        tokens,
        w_query[0],
        w_key[0],
        w_value[0],
        w_out[0],
        cache_keys[0].reshape(cached, BLOCK, WIDTH),
        cache_values[0].reshape(cached, BLOCK, WIDTH),
    )
    return jnp.where(lax.axis_index("sec") == 0, fresh_tokens, shifted)


def solution(mesh):
    in_specs = (
        P("sec", "head"),
        P(None, "head"),
        P("sec", None, None),
        P("sec", None, None),
        P("sec", None),
        P("sec", None),
        P("sec", None, "head"),
        P("sec", None, "head"),
        P("sec", None, "head"),
        P("sec", None, "head"),
        P("sec", None, "head"),
        P("sec", None, "head"),
    )
    return jax.shard_map(
        body, mesh=mesh, in_specs=in_specs, out_specs=P("sec", "head"), check_vma=False
    )
```

time: 153 us -> 66 us (0.43)
  the two profiles are of different devices: /device:TPU:2 before, /device:TPU:1 now
where the time goes in v1:
time: 66 us; the launch traced here: 65.9 us
  Pallas kernels  65.1 us (99%)
  other arithmetic  0.75 us (1%)
    pallas_call x1, Pallas kernels, body(): pl.pallas_call(functools.partial(kernel, sections, chips), out_shape=jax....  65.1 us

profile of v1, /device:TPU:1, one launch (start us, length us, event | category | flops | bytes accessed | tf_op | source)
XLA Modules:
  0.0 65.9 jit_solution(8643563705356507400)
XLA Ops:
  0.0 0.0 copy-start
  0.0 65.1 %shard_map.118 = bf16[1024,128]{1,0:T(8,128)(2,1)} custom-call(s32[4,16]{1,0:T(4,128)} %bitcast.14, s32[4,128]{1,0:T(4,128)} %bitcast.15, f32[1,2048]{1,0:T(1,128)} %gain_hbm.1, bf16[1,2048]{1,0:T(2,128)(2,1)} %router_hbm.1, bf16[1024,128]{1,0:T(8,128)(2,1)} %tokens_hbm.1, bf16[2048,128]{1,0:T(8,128)(2,1)} %bitcast.10, bf16[2048,128]{1,0:T(8,128)(2,1)} %bitcast.11, ...), custom_call_target="tpu_custom_call" | custom-call | tf_op jit(solution)/shard_map/pallas_call | solution.py:321
  65.1 0.0 copy-done
  65.1 0.7 %broadcast_select_fusion = bf16[1024,128]{1,0:T(8,128)(2,1)} fusion(bf16[1024,128]{1,0:T(8,128)(2,1)S(1)} %copy-done, bf16[1024,128]{1,0:T(8,128)(2,1)} %shard_map.118, pred[]{:T(512)S(6)} %eq.3), kind=kLoop, calls=%fused_computation | loop fusion | flops 131072 | bytes 786433 | tf_op jit(solution)/shard_map/jit(_where)/select_n | solution.py:369
Async XLA Ops:
  0.0 65.1 %copy-start = (bf16[1024,128]{1,0:T(8,128)(2,1)S(1)}, bf16[1024,128]{1,0:T(8,128)(2,1)}, u32[]{:S(2)}) copy-start(bf16[1024,128]{1,0:T(8,128)(2,1)} %param.13) | copy-start | bytes 786436

commit v2 on v1

--- a/solution.py
+++ b/solution.py
@@ -11,6 +11,8 @@
 BLOCK = 128
 WIDTH = 128
 MESH = pl.DeviceIdType.MESH
+OWN = ((1,), (1, 2))
+ONWARD = ({1: (2,), 2: (3, 4)}, {2: (3, 4)})
 F32 = jnp.float32
 BF16 = jnp.bfloat16
 
@@ -71,36 +73,34 @@
     head = lax.axis_index("head")
     chip = head // 2
     core = head % 2
-    up = ((chip + 1) % chips) * 2 + core
-    down = ((chip + chips - 1) % chips) * 2 + core
+
+    def at(off):
+        return ((chip + chips + off) % chips) * 2 + core
+
     pair = chip * 2 + 1 - core
     after = (sec + 1) % sections
     before = (sec + sections - 1) % sections
 
-    loads = [
-        pltpu.make_async_copy(a, b, load_sem.at[i])
-        for i, (a, b) in enumerate(
-            (
-                (route_hbm, route),
-                (tokens_hbm, tokens),
-                (router_hbm, router),
-                (gain_hbm, gain),
-                (wq_hbm, wcat.at[:, pl.ds(0, WIDTH)]),
-                (wk_hbm, wcat.at[:, pl.ds(WIDTH, WIDTH)]),
-                (wv_hbm, wcat.at[:, pl.ds(2 * WIDTH, WIDTH)]),
-                (ck_hbm, ck),
-                (cv_hbm, cv),
-                (wo_hbm, wo),
-            )
-        )
+    def rows_of(g):
+        return pl.ds(g * group_rows, group_rows)
+
+    def load(i, source, target):
+        copy = pltpu.make_async_copy(source, target, load_sem.at[i])
+        copy.start()
+        return copy
+
+    route_load = load(0, route_hbm, route)
+    token_loads = [
+        load(1 + g, tokens_hbm.at[rows_of(g)], tokens.at[rows_of(g)])
+        for g in range(groups)
     ]
-    for load in loads:
-        load.start()
 
     barrier = pltpu.get_barrier_semaphore()
     for there in (
-        {"head": up},
-        {"head": down},
+        {"head": at(1)},
+        {"head": at(-1)},
+        {"head": at(2)},
+        {"head": at(-2)},
         {"head": pair},
         {"sec": after},
         {"sec": before},
@@ -109,17 +109,17 @@
 
     bufs = (xg, ag)
 
-    def ring_copy(p, g, slot, hop, way):
+    def message(p, g, way, reach, dist, slot):
         ref = bufs[p].at[g, slot]
-        if hop == half:
+        if reach == half:
             ref = ref.at[pl.ds(way * (routed // 2), routed // 2)]
-        i = 2 * (hop - 1) + way
+        i = 2 * (reach - 1) + way
         return pltpu.make_async_remote_copy(
             src_ref=ref,
             dst_ref=ref,
             send_sem=ring_send.at[p, g, i],
             recv_sem=ring_recv.at[p, g, i],
-            device_id={"head": up if way == 0 else down},
+            device_id={"head": at(dist if way == 0 else -dist)},
             device_id_type=MESH,
         )
 
@@ -134,40 +134,45 @@
             device_id_type=MESH,
         )
 
-    def arrived(hop, way):
-        off = chips - hop if way == 0 else hop
-        return ((chip + off) % chips) * 2 + core
+    def arrived(reach, way):
+        return at(-reach if way == 0 else reach)
 
     def send_own(p, g):
+        for reach in OWN[p]:
+            for way in (0, 1):
+                message(p, g, way, reach, reach, head).start()
+        pair_copy(p, g, head, 0).start()
+
+    def step(p, g, reach):
         for way in (0, 1):
-            ring_copy(p, g, head, 1, way).start()
-        pair_copy(p, g, head, 0).start()
-
-    def ring_step(p, g, hop):
-        for way in (0, 1):
-            slot = arrived(hop, way)
-            ring_copy(p, g, slot, hop, way).wait_recv()
-            if hop < half:
-                ring_copy(p, g, slot, hop + 1, way).start()
-                pair_copy(p, g, slot, 2 * hop - 1 + way).start()
-        if hop == half:
-            pair_copy(p, g, arrived(hop, 0), 2 * half - 1).start()
+            slot = arrived(reach, way)
+            message(p, g, way, reach, 1, slot).wait_recv()
+            for farther in ONWARD[p].get(reach, ()):
+                message(p, g, way, farther, farther - reach, slot).start()
+            if reach < half:
+                pair_copy(p, g, slot, 2 * reach - 1 + way).start()
+        if reach == half:
+            pair_copy(p, g, arrived(reach, 0), 2 * half - 1).start()
+
+    def steps(p, g, *reaches):
+        for reach in reaches:
+            step(p, g, reach)
 
     def pair_wait(p, g):
         for i in range(2 * half):
             pair_copy(p, g, pair, i).wait_recv()
 
     def drain(p, g):
-        for hop in range(1, half + 1):
+        for reach in range(1, half + 1):
             for way in (0, 1):
-                ring_copy(p, g, head, hop, way).wait_send()
+                message(p, g, way, reach, 1, head).wait_send()
         for i in range(2 * half):
             pair_copy(p, g, head, i).wait_send()
 
     def next_copy(g):
         return pltpu.make_async_remote_copy(
-            src_ref=result.at[pl.ds(g * group_rows, group_rows)],
-            dst_ref=out_ref.at[pl.ds(g * group_rows, group_rows)],
+            src_ref=result.at[rows_of(g)],
+            dst_ref=out_ref.at[rows_of(g)],
             send_sem=next_send.at[g],
             recv_sem=next_recv.at[g],
             device_id={"sec": after},
@@ -177,15 +182,15 @@
     def pick(g):
         chosen = route[g : g + 1, :]
         rows = lax.broadcasted_iota(jnp.int32, (group_rows, routed), 0)
-        one_hot = jnp.where(rows == chosen, 1.0, 0.0).astype(F32)
-        here = one_hot.astype(BF16)
+        here = jnp.where(rows == chosen, 1.0, 0.0).astype(BF16)
         place[g] = here
-        mine = tokens[pl.ds(g * group_rows, group_rows), :]
-        xg[g, head] = dot(here, mine, ((0,), (0,))).astype(BF16)
-        used = jnp.max(one_hot, axis=1, keepdims=True)
-        passed[pl.ds(g * group_rows, group_rows), :] = jnp.where(
-            used > 0.0, 0.0, mine.astype(F32)
-        ).astype(BF16)
+        token_loads[g].wait()
+        xg[g, head] = dot(here, tokens[rows_of(g), :], ((0,), (0,))).astype(BF16)
+
+    def pass_rest(g):
+        used = jnp.max(place[g].astype(F32), axis=1, keepdims=True)
+        mine = tokens[rows_of(g), :].astype(F32)
+        passed[rows_of(g), :] = jnp.where(used > 0.0, 0.0, mine).astype(BF16)
 
     def project(g):
         total = jnp.zeros((routed, WIDTH), F32)
@@ -246,46 +251,77 @@
         ag[g, head] = jnp.where(first, ratio[:routed], ratio[routed:]).astype(BF16)
 
     def finish(g):
+        pair_wait(1, g)
         attended = jnp.concatenate([ag[g, s] for s in range(shards)], axis=1)
         branch = dot(attended, wo[...])
         updated = (xg[g, head].astype(F32) + gates[g] * branch).astype(BF16)
-        rows = pl.ds(g * group_rows, group_rows)
         moved = dot(place[g], updated)
-        result[rows, :] = (moved + passed[rows, :].astype(F32)).astype(BF16)
+        rest = passed[rows_of(g), :].astype(F32)
+        result[rows_of(g), :] = (moved + rest).astype(BF16)
         next_copy(g).start()
 
-    loads[0].wait()
-    loads[1].wait()
-    for g in range(groups):
+    def compute(g):
+        pair_wait(0, g)
+        attend(g, project(g))
+        send_own(1, g)
+
+    route_load.wait()
+    pick(0)
+    pl.semaphore_wait(barrier, 7)
+    send_own(0, 0)
+    for g in range(1, groups):
         pick(g)
-    pl.semaphore_wait(barrier, 5)
-    for g in range(groups):
         send_own(0, g)
 
-    loads[2].wait()
+    router_load = load(5, router_hbm, router)
+    loads = [
+        load(6 + i, source, target)
+        for i, (source, target) in enumerate(
+            (
+                (gain_hbm, gain),
+                (wq_hbm, wcat.at[:, pl.ds(0, WIDTH)]),
+                (wk_hbm, wcat.at[:, pl.ds(WIDTH, WIDTH)]),
+                (wv_hbm, wcat.at[:, pl.ds(2 * WIDTH, WIDTH)]),
+                (ck_hbm, ck),
+                (cv_hbm, cv),
+                (wo_hbm, wo),
+            )
+        )
+    ]
+    router_load.wait()
     for s in range(shards):
         lanes = slice(s * WIDTH, (s + 1) * WIDTH)
         wide = jnp.broadcast_to(router[:, lanes].astype(F32), (WIDTH, WIDTH))
         wcat[lanes, 3 * WIDTH :] = jnp.transpose(wide).astype(BF16)
-
-    for hop in range(1, half + 1):
-        for g in range(groups):
-            ring_step(0, g, hop)
-    for load in loads[3:]:
-        load.wait()
-
-    for t in range(groups + half):
-        if t < groups:
-            pair_wait(0, t)
-            attend(t, project(t))
-            send_own(1, t)
-        for g in range(groups):
-            if 1 <= t - g <= half:
-                ring_step(1, g, t - g)
-        done = t - half
-        if done >= 0:
-            pair_wait(1, done)
-            finish(done)
+    for g in range(groups):
+        step(0, g, 1)
+    for g in range(groups):
+        pass_rest(g)
+    for g in range(groups):
+        step(0, g, 2)
+    for copy in loads:
+        copy.wait()
+
+    steps(0, 0, 3, 4)
+    steps(0, 1, 3, 4)
+    compute(0)
+    steps(0, 2, 3, 4)
+    compute(1)
+    steps(0, 3, 3, 4)
+    compute(2)
+    steps(1, 0, 1, 2)
+    compute(3)
+    steps(1, 1, 1, 2)
+    steps(1, 0, 3, 4)
+    steps(1, 2, 1, 2)
+    steps(1, 1, 3, 4)
+    finish(0)
+    steps(1, 3, 1, 2)
+    steps(1, 2, 3, 4)
+    finish(1)
+    steps(1, 3, 3, 4)
+    finish(2)
+    finish(3)
 
     for g in range(groups):
         drain(0, g)
@@ -342,7 +378,7 @@
             pltpu.VMEM((groups, rows // groups, routed), BF16),
             pltpu.VMEM((rows, WIDTH), BF16),
             pltpu.VMEM((rows, WIDTH), BF16),
-            dma((10,)),
+            dma((13,)),
             dma((2, groups, 2 * half)),
             dma((2, groups, 2 * half)),
             dma((2, groups, 2 * half)),

time: 66 us -> 58 us (0.88)
  Pallas kernels: 65.1 us -> 57 us
    pallas_call x1, Pallas kernels: 65.1 us -> 57 us  [body(): pl.pallas_call(functools.partial(kernel, sections, chips), out_shape=jax....]
where the time goes in v2:
time: 58 us; the launch traced here: 57.8 us
  Pallas kernels  57 us (98%)
  other arithmetic  0.75 us (1%)
    pallas_call x1, Pallas kernels, body(): pl.pallas_call(functools.partial(kernel, sections, chips), out_shape=jax....  57 us

profile of v2, /device:TPU:1, one launch (start us, length us, event | category | flops | bytes accessed | tf_op | source)
XLA Modules:
  0.0 57.8 jit_solution(8518827020563735429)
XLA Ops:
  0.0 0.0 copy-start
  0.0 57.0 %shard_map.118 = bf16[1024,128]{1,0:T(8,128)(2,1)} custom-call(s32[4,16]{1,0:T(4,128)} %bitcast.14, s32[4,128]{1,0:T(4,128)} %bitcast.15, f32[1,2048]{1,0:T(1,128)} %gain_hbm.1, bf16[1,2048]{1,0:T(2,128)(2,1)} %router_hbm.1, bf16[1024,128]{1,0:T(8,128)(2,1)} %tokens_hbm.1, bf16[2048,128]{1,0:T(8,128)(2,1)} %bitcast.10, bf16[2048,128]{1,0:T(8,128)(2,1)} %bitcast.11, ...), custom_call_target="tpu_custom_call" | custom-call | tf_op jit(solution)/shard_map/pallas_call | solution.py:357
  57.0 0.0 copy-done
  57.0 0.7 %broadcast_select_fusion = bf16[1024,128]{1,0:T(8,128)(2,1)} fusion(bf16[1024,128]{1,0:T(8,128)(2,1)S(1)} %copy-done, bf16[1024,128]{1,0:T(8,128)(2,1)} %shard_map.118, pred[]{:T(512)S(6)} %eq.3), kind=kLoop, calls=%fused_computation | loop fusion | flops 131072 | bytes 786433 | tf_op jit(solution)/shard_map/jit(_where)/select_n | solution.py:405
Async XLA Ops:
  0.0 57.0 %copy-start = (bf16[1024,128]{1,0:T(8,128)(2,1)S(1)}, bf16[1024,128]{1,0:T(8,128)(2,1)}, u32[]{:S(2)}) copy-start(bf16[1024,128]{1,0:T(8,128)(2,1)} %param.13) | copy-start | bytes 786436

commit v3 on v2

--- a/solution.py
+++ b/solution.py
@@ -11,8 +11,8 @@
 BLOCK = 128
 WIDTH = 128
 MESH = pl.DeviceIdType.MESH
-OWN = ((1,), (1, 2))
-ONWARD = ({1: (2,), 2: (3, 4)}, {2: (3, 4)})
+OWN = (1, 2)
+ONWARD = {2: (3, 4)}
 F32 = jnp.float32
 BF16 = jnp.bfloat16
 
@@ -48,6 +48,7 @@
     ag,
     normed,
     scores,
+    queries,
     klocal,
     vlocal,
     gates,
@@ -138,7 +139,7 @@
         return at(-reach if way == 0 else reach)
 
     def send_own(p, g):
-        for reach in OWN[p]:
+        for reach in OWN:
             for way in (0, 1):
                 message(p, g, way, reach, reach, head).start()
         pair_copy(p, g, head, 0).start()
@@ -147,7 +148,7 @@
         for way in (0, 1):
             slot = arrived(reach, way)
             message(p, g, way, reach, 1, slot).wait_recv()
-            for farther in ONWARD[p].get(reach, ()):
+            for farther in ONWARD.get(reach, ()):
                 message(p, g, way, farther, farther - reach, slot).start()
             if reach < half:
                 pair_copy(p, g, slot, 2 * reach - 1 + way).start()
@@ -193,26 +194,31 @@
         passed[rows_of(g), :] = jnp.where(used > 0.0, 0.0, mine).astype(BF16)
 
     def project(g):
+        pair_wait(0, g)
         total = jnp.zeros((routed, WIDTH), F32)
         for s in range(shards):
             x = xg[g, s].astype(F32)
             total += x * x
         mean = jnp.sum(total, axis=1, keepdims=True) * (1.0 / width)
         scale = lax.rsqrt(mean + 1e-05)
+        gate = jnp.zeros((routed, WIDTH), F32)
         for s in range(shards):
             lanes = slice(s * WIDTH, (s + 1) * WIDTH)
             x = xg[g, s].astype(F32)
-            normed[:, lanes] = (x * scale * gain[:, lanes]).astype(BF16)
+            n = (x * scale * gain[:, lanes]).astype(BF16)
+            normed[:, lanes] = n
+            gate += n.astype(F32) * router[:, lanes].astype(F32)
         y = dot(normed[...], wcat[...])
-        gates[g] = jax.nn.sigmoid(y[:, 3 * WIDTH :])
+        logit = jnp.sum(gate, axis=1, keepdims=True)
+        gates[g] = jnp.broadcast_to(jax.nn.sigmoid(logit), (routed, WIDTH))
         klocal[g] = y[:, WIDTH : 2 * WIDTH].astype(BF16)
-        vlocal[g] = y[:, 2 * WIDTH : 3 * WIDTH].astype(BF16)
-        return y[:, :WIDTH].astype(BF16)
-
-    def attend(g, q):
+        vlocal[g] = y[:, 2 * WIDTH :].astype(BF16)
+        queries[g] = y[:, :WIDTH].astype(BF16)
+
+    def attend(g):
         lane = lax.broadcasted_iota(jnp.int32, (routed, WIDTH), 1)
         first = lane < HEAD_DIM
-        qs = q.astype(F32) * 0.125
+        qs = queries[g].astype(F32) * 0.125
         both = jnp.concatenate(
             [jnp.where(first, qs, 0.0), jnp.where(first, 0.0, qs)], axis=0
         ).astype(BF16)
@@ -260,24 +266,21 @@
         result[rows_of(g), :] = (moved + rest).astype(BF16)
         next_copy(g).start()
 
-    def compute(g):
-        pair_wait(0, g)
-        attend(g, project(g))
+    def answer(g):
+        attend(g)
         send_own(1, g)
 
     route_load.wait()
     pick(0)
     pl.semaphore_wait(barrier, 7)
     send_own(0, 0)
-    for g in range(1, groups):
-        pick(g)
-        send_own(0, g)
-
-    router_load = load(5, router_hbm, router)
+    pick(1)
+    send_own(0, 1)
     loads = [
-        load(6 + i, source, target)
+        load(5 + i, source, target)
         for i, (source, target) in enumerate(
             (
+                (router_hbm, router),
                 (gain_hbm, gain),
                 (wq_hbm, wcat.at[:, pl.ds(0, WIDTH)]),
                 (wk_hbm, wcat.at[:, pl.ds(WIDTH, WIDTH)]),
@@ -288,39 +291,43 @@
             )
         )
     ]
-    router_load.wait()
-    for s in range(shards):
-        lanes = slice(s * WIDTH, (s + 1) * WIDTH)
-        wide = jnp.broadcast_to(router[:, lanes].astype(F32), (WIDTH, WIDTH))
-        wcat[lanes, 3 * WIDTH :] = jnp.transpose(wide).astype(BF16)
-    for g in range(groups):
-        step(0, g, 1)
-    for g in range(groups):
-        pass_rest(g)
-    for g in range(groups):
-        step(0, g, 2)
+    pick(2)
+    pick(3)
+    steps(0, 0, 1, 2)
+    send_own(0, 2)
+    steps(0, 1, 1, 2)
+    send_own(0, 3)
+    steps(0, 0, 3, 4)
     for copy in loads:
         copy.wait()
-
-    steps(0, 0, 3, 4)
+    project(0)
+    steps(0, 2, 1, 2)
+    answer(0)
     steps(0, 1, 3, 4)
-    compute(0)
+    project(1)
+    steps(0, 3, 1, 2)
+    answer(1)
     steps(0, 2, 3, 4)
-    compute(1)
+    project(2)
+    steps(1, 0, 1, 2)
+    answer(2)
     steps(0, 3, 3, 4)
-    compute(2)
-    steps(1, 0, 1, 2)
-    compute(3)
+    project(3)
     steps(1, 1, 1, 2)
+    answer(3)
+    pass_rest(0)
+    pass_rest(1)
     steps(1, 0, 3, 4)
     steps(1, 2, 1, 2)
     steps(1, 1, 3, 4)
+    pass_rest(2)
+    pass_rest(3)
     finish(0)
     steps(1, 3, 1, 2)
+    finish(1)
     steps(1, 2, 3, 4)
-    finish(1)
+    finish(2)
     steps(1, 3, 3, 4)
-    finish(2)
     finish(3)
 
     for g in range(groups):
@@ -364,7 +371,7 @@
             pltpu.VMEM((1, width), F32),
             pltpu.VMEM((1, width), BF16),
             pltpu.VMEM((rows, WIDTH), BF16),
-            pltpu.VMEM((width, 4 * WIDTH), BF16),
+            pltpu.VMEM((width, 3 * WIDTH), BF16),
             pltpu.VMEM((width, WIDTH), BF16),
             pltpu.VMEM((cached, BLOCK, WIDTH), BF16),
             pltpu.VMEM((cached, BLOCK, WIDTH), BF16),
@@ -372,6 +379,7 @@
             pltpu.VMEM((groups, shards, routed, WIDTH), BF16),
             pltpu.VMEM((routed, width), BF16),
             pltpu.VMEM((2 * routed, picked + groups * routed), F32),
+            pltpu.VMEM((groups, routed, WIDTH), BF16),
             pltpu.VMEM((groups, routed, WIDTH), BF16),
             pltpu.VMEM((groups, routed, WIDTH), BF16),
             pltpu.VMEM((groups, routed, WIDTH), F32),

time: 58 us -> 57.2 us (0.986)
  Pallas kernels: 57 us -> 56.3 us
    pallas_call x1, Pallas kernels: 57 us -> 56.3 us  [body(): pl.pallas_call(functools.partial(kernel, sections, chips), out_shape=jax....]
where the time goes in v3:
time: 57.2 us; the launch traced here: 57 us
  Pallas kernels  56.3 us (98%)
  other arithmetic  0.75 us (1%)
    pallas_call x1, Pallas kernels, body(): pl.pallas_call(functools.partial(kernel, sections, chips), out_shape=jax....  56.3 us

profile of v3, /device:TPU:1, one launch (start us, length us, event | category | flops | bytes accessed | tf_op | source)
XLA Modules:
  0.0 57.0 jit_solution(13870224289414044101)
XLA Ops:
  0.0 0.0 copy-start
  0.0 56.3 %shard_map.118 = bf16[1024,128]{1,0:T(8,128)(2,1)} custom-call(s32[4,16]{1,0:T(4,128)} %bitcast.14, s32[4,128]{1,0:T(4,128)} %bitcast.15, f32[1,2048]{1,0:T(1,128)} %gain_hbm.1, bf16[1,2048]{1,0:T(2,128)(2,1)} %router_hbm.1, bf16[1024,128]{1,0:T(8,128)(2,1)} %tokens_hbm.1, bf16[2048,128]{1,0:T(8,128)(2,1)} %bitcast.10, bf16[2048,128]{1,0:T(8,128)(2,1)} %bitcast.11, ...), custom_call_target="tpu_custom_call" | custom-call | tf_op jit(solution)/shard_map/pallas_call | solution.py:364
  56.3 0.0 copy-done
  56.3 0.7 %broadcast_select_fusion = bf16[1024,128]{1,0:T(8,128)(2,1)} fusion(bf16[1024,128]{1,0:T(8,128)(2,1)S(1)} %copy-done, bf16[1024,128]{1,0:T(8,128)(2,1)} %shard_map.118, pred[]{:T(512)S(6)} %eq.3), kind=kLoop, calls=%fused_computation | loop fusion | flops 131072 | bytes 786433 | tf_op jit(solution)/shard_map/jit(_where)/select_n | solution.py:413
Async XLA Ops:
  0.0 56.3 %copy-start = (bf16[1024,128]{1,0:T(8,128)(2,1)S(1)}, bf16[1024,128]{1,0:T(8,128)(2,1)}, u32[]{:S(2)}) copy-start(bf16[1024,128]{1,0:T(8,128)(2,1)} %param.13) | copy-start | bytes 786436
